TPU v7x, 32 devices: a whole 2x2x4 slice. The times are simulated.
32 devices in a mesh: chan: 16 (over z, y, x), win: 2 (over core).
Axes of the slice: x: 2, y: 2, z: 4, core: 2. Of those that a mesh axis runs over, the one named last changes fastest.
Arguments:
- samples: bfloat16 [2, 2048, 1024], P('win', 'chan'), may hold values from -12 to 12
- pair_tiles: int32 [128, 3], replicated, may hold values from -1 to 15, as said below
Outputs:
- stacks: float32 [128, 64, 128, 128], P('chan', 'win')
Inputs may be any that keep to these rules, and one draw needn't show every extreme that they name: Each row of pair_tiles is (a, b, o) with a <= b <= a + 2 and b < 16 and b - 2 <= o <= a + 2, or (-1, -1, -1) for an empty slot. Rows k * 8 to (k + 1) * 8 - 1 hold the tiles of owner k, live rows first. Every pair of blocks with a <= b <= a + 2 is listed exactly once, and some owner has 8 tiles.
All inputs are finite; a program needn't handle non-finite values.
Results may differ from a plain program's by a relative error of at most 0.007.
Values may be sent and summed in bfloat16 or wider, within the bound.
No kernel may reach another device: no remote copies, remote signals or barrier semaphores. Data moves between devices by JAX's collectives and lax.ppermute only.
A program may use at most 64 MiB of HBM per device.

v0:
```python
import functools
import math

import jax
import jax.numpy as jnp
from jax import lax
from jax.experimental import pallas as pl
from jax.experimental.pallas import tpu as pltpu
from jax.sharding import PartitionSpec as P

NSAMP = 1024
FREQS = 512
VIRTUAL_SOURCES = 64
LAGS = 128
TILE_CAP = 8
CH = 128
LANES = 128
RE_CHUNKS = FREQS // LANES
CHUNKS = 2 * RE_CHUNKS
FAR = 3
NEARBY = 5
ROWS = 8
QUARTER = NSAMP // 4
VMEM_BYTES = 16 * 1024 * 1024
COSTS = 1, 16, 16, 16
PART = 8


def turns(steps):
    angles = (steps & (NSAMP - 1)).astype(jnp.float32) * (2.0 * math.pi / NSAMP)
    return jnp.cos(angles), jnp.sin(angles)


def turned(rows, slow, fast):
    slow_cos, slow_sin = (part[:, None, :] for part in turns(slow))
    fast_cos, fast_sin = (part[None] for part in turns(fast))
    cos = (slow_cos * fast_cos - slow_sin * fast_sin).reshape(rows, LANES)
    sin = (slow_sin * fast_cos + slow_cos * fast_sin).reshape(rows, LANES)
    return cos, sin


def counts(shape, dimension):
    return lax.broadcasted_iota(jnp.int32, shape, dimension)


def forward_kernel(table):
    blocks = QUARTER // ROWS
    for c in range(RE_CHUNKS):
        slow = counts((blocks, LANES), 0) * ROWS * (counts((blocks, LANES), 1) + c * LANES)
        fast = counts((ROWS, LANES), 0) * (counts((ROWS, LANES), 1) + c * LANES)
        cos, sin = turned(QUARTER, slow, fast)
        table[c, :, :LANES] = cos.astype(jnp.bfloat16)
        table[c, :, LANES:] = (-sin).astype(jnp.bfloat16)


def forward_table():
    return pl.pallas_call(
        forward_kernel,
        out_shape=jax.ShapeDtypeStruct((RE_CHUNKS, QUARTER, 2 * LANES), jnp.bfloat16),
        out_specs=pl.BlockSpec(memory_space=pltpu.VMEM),
        compiler_params=pltpu.CompilerParams(vmem_limit_bytes=VMEM_BYTES),
        name="forward_table",
    )()


def write_inverse(table, scale):
    blocks = LAGS // ROWS
    for c in range(RE_CHUNKS):
        lag = counts((blocks, LANES), 0) * ROWS - LAGS // 2 + NSAMP
        slow = lag * (counts((blocks, LANES), 1) + c * LANES)
        fast = counts((ROWS, LANES), 0) * (counts((ROWS, LANES), 1) + c * LANES)
        cos, sin = turned(LAGS, slow, fast)
        table[c] = (cos * scale).astype(jnp.bfloat16)
        table[RE_CHUNKS + c] = (sin * -scale).astype(jnp.bfloat16)


def coded_slots(pairs, device, late):
    def place_of(block):
        apart = jnp.abs(block - device)
        far = jnp.where(apart == 1, FAR, FAR + 1)
        near = jnp.where(block == (device ^ 1), 1, jnp.where(block == (device ^ 2), 2, far))
        return jnp.where(apart == 0, 0, near)

    a, b, owner = pairs[0:1, :], pairs[1:2, :], pairs[2:3, :]
    a, b = place_of(a), place_of(b)
    last = jnp.maximum(a, b)
    far = jnp.where((a == late) | (b == late), 4, 3)
    phase = jnp.where(last == 0, 1, jnp.where(last < FAR, 2, far))
    slot = counts(owner.shape, 1) - device * TILE_CAP
    code = jnp.where(owner >= 0, phase + 8 * (5 * a + b), 0) << (8 * (slot & 3))
    words = [
        jnp.sum(jnp.where((slot >= 4 * q) & (slot < 4 * q + 4), code, 0)) for q in range(2)
    ]
    return lambda j: (jnp.where(j < 4, words[0], words[1]) >> (8 * (j & 3))) & 255


def whiten_kernel(samples, table, out_ref, spectra):
    rows = [samples[0, :, q * QUARTER : (q + 1) * QUARTER] for q in range(4)]
    bins = counts((QUARTER, LANES), 1)
    sign = (1 - 2 * (bins & 1)).astype(jnp.float32).astype(jnp.bfloat16)
    by_cos = ((1 - (bins & 1)) * (1 - (bins & 2))).astype(jnp.float32).astype(jnp.bfloat16)
    by_sin = ((bins & 1) * (1 - (bins & 2))).astype(jnp.float32).astype(jnp.bfloat16)
    total = jnp.zeros((CH, LANES), jnp.float32)
    for c in range(RE_CHUNKS):
        cos, sin = table[c, :, :LANES], table[c, :, LANES:]
        next_cos = by_cos * cos + by_sin * sin
        next_sin = by_cos * sin - by_sin * cos
        quarters = (cos, sin), (next_cos, next_sin), (sign * cos, sign * sin), (
            sign * next_cos, sign * next_sin,
        )
        part = jnp.zeros((CH, 2 * LANES), jnp.float32)
        for q in range(4):
            part = part + jnp.dot(
                rows[q], jnp.concatenate(quarters[q], axis=1), preferred_element_type=jnp.float32
            )
        spectra[c] = part
        real, imag = part[:, :LANES], part[:, LANES:]
        total = total + (real * real + imag * imag)
    level = jnp.sum(total, axis=1, keepdims=True) * (0.5 / FREQS) + 1e-06
    for c in range(RE_CHUNKS):
        real, imag = spectra[c, :, :LANES], spectra[c, :, LANES:]
        factor = lax.rsqrt(real * real + imag * imag + level)
        out_ref[c] = (real * factor).astype(jnp.bfloat16)
        out_ref[RE_CHUNKS + c] = (imag * factor).astype(jnp.bfloat16)


def whiten(samples):
    return pl.pallas_call(
        whiten_kernel,
        out_shape=jax.ShapeDtypeStruct((CHUNKS, CH, LANES), jnp.bfloat16),
        in_specs=[pl.BlockSpec(memory_space=pltpu.VMEM)] * 2,
        out_specs=pl.BlockSpec(memory_space=pltpu.VMEM),
        scratch_shapes=[pltpu.VMEM((RE_CHUNKS, CH, 2 * LANES), jnp.float32)],
        compiler_params=pltpu.CompilerParams(vmem_limit_bytes=VMEM_BYTES),
        name="whiten",
    )(samples, forward_table())


def cross_chunk(source, target, windows, chunk, s):
    real = imag = None
    for w in range(windows):
        a_re = jnp.broadcast_to(source[w, chunk, pl.ds(s, 1), :], (CH, LANES))
        a_im = jnp.broadcast_to(source[w, RE_CHUNKS + chunk, pl.ds(s, 1), :], (CH, LANES))
        a_re, a_im = a_re.astype(jnp.bfloat16), a_im.astype(jnp.bfloat16)
        b_re, b_im = target[w, chunk], target[w, RE_CHUNKS + chunk]
        re = a_re * b_re + a_im * b_im
        im = a_im * b_re - a_re * b_im
        real = re if real is None else real + re
        imag = im if imag is None else imag + im
    return jnp.concatenate([real, imag], axis=1)


def tile_kernel(config, pairs, *refs):
    phase, windows, sources, scale, first, clears, layout = config
    exact = math.frexp(scale)[0] == 0.5
    count = sum(held for _, _, held in layout)
    given = 0 if first else 1
    blocks = refs[given : given + count]
    member = lax.axis_index("win")
    late = FAR + 1 - member if lax.axis_size("win") == 2 else NEARBY
    code_of = coded_slots(pairs, lax.axis_index("chan"), late)
    if first:
        out, table, target, source, rows, tiles, zeros, out_sems, zero_sems = refs[count:]
        write_inverse(table, scale if exact else 1.0)
    else:
        table = refs[0]
        out, target, source, rows, tiles, zeros, out_sems, zero_sems = refs[2 + count :]
    span = sources * CH // VIRTUAL_SOURCES
    parts = [(at, min(PART, sources - at)) for at in range(0, sources, PART)]

    def clear(j):
        return pltpu.make_async_copy(zeros, out.at[j], zero_sems.at[j])

    def each_empty(act):
        @pl.loop(0, TILE_CAP)
        def _(j):
            @pl.when(code_of(j) == 0)
            def _():
                act(j)

    if clears:
        zeros[...] = jnp.zeros_like(zeros)
        each_empty(lambda j: clear(j).start())

    def each_window(place, act):
        position = 0
        for known, kind, held in layout:
            held = blocks[position : position + held]
            position += len(held)
            if kind == "all":

                @pl.when(place == known)
                def _():
                    for w in range(windows):
                        act(w, held[0].at[w])

                continue
            for i, ref in enumerate(held):
                nearer = (1 - member) if i else member

                @pl.when(place == (known + nearer if kind == "two" else known))
                def _():
                    act(nearer, ref if kind == "own" else ref.at[0])
                    if kind == "two":
                        act(1 - nearer, ref.at[1])

    def leave(parity, j, p):
        at, size = parts[p]
        part = pl.ds(at, size)
        return pltpu.make_async_copy(
            tiles.at[parity, part], out.at[j, part], out_sems.at[parity, p]
        )

    def left(parity):
        for p in range(len(parts)):
            leave(parity, 0, p).wait()

    def take_source(w, ref):
        for c in range(CHUNKS):
            rows[c] = ref[c, pl.ds(pl.multiple_of(member * span, span), span), :].astype(
                jnp.float32
            )
            source[w, c] = rows[c, pl.ds(0, sources, stride=CH // VIRTUAL_SOURCES), :]

    def take_target(w, ref):
        target[w] = ref[...]

    def one_tile(j, place_a, place_b, done):
        parity = done & 1
        each_window(place_a, take_source)
        each_window(place_b, take_target)

        @pl.when(done >= 2)
        def _():
            left(parity)

        for p, (at, size) in enumerate(parts):
            for s in range(at, at + size):
                stacked = jnp.zeros((LAGS, CH), jnp.float32)
                for c in range(RE_CHUNKS):
                    cross = cross_chunk(source, target, windows, c, s)
                    lags = jnp.concatenate([table[c], table[RE_CHUNKS + c]], axis=1)
                    stacked = stacked + lax.dot_general(
                        lags, cross, (((1,), (1,)), ((), ())), preferred_element_type=jnp.float32
                    )
                tiles[parity, s] = stacked if exact else stacked * scale
            leave(parity, j, p).start()

    def one_slot(j, done):
        code = code_of(j)
        mine = (code & 7) == phase
        places = code >> 3
        place_a = lax.div(places, 5)

        @pl.when(mine)
        def _():
            one_tile(j, place_a, places - 5 * place_a, done)

        return done + mine.astype(jnp.int32)

    done = lax.fori_loop(0, TILE_CAP, one_slot, 0)
    for back in (1, 2):

        @pl.when(done >= back)
        def _():
            left((done - back) & 1)

    if clears:
        each_empty(lambda j: clear(j).wait())


def tile_call(phase, known, layout, blocks, out, sources, windows, scale, clears=False):
    first = out is None
    config = (phase, windows, sources, scale, first, clears, layout)
    held = pl.BlockSpec(memory_space=pltpu.VMEM)
    anywhere = pl.BlockSpec(memory_space=pl.ANY)
    operands = [*known, *blocks] + ([] if first else [out])
    specs = [held] * (len(operands) - (not first)) + ([] if first else [anywhere])
    out_shape = [jax.ShapeDtypeStruct((TILE_CAP, sources, LAGS, CH), jnp.float32)]
    out_specs = [anywhere]
    scratch_shapes = [
        pltpu.VMEM((windows, CHUNKS, CH, LANES), jnp.bfloat16),
        pltpu.VMEM((windows, CHUNKS, sources, LANES), jnp.float32),
        pltpu.VMEM((CHUNKS, sources * CH // VIRTUAL_SOURCES, LANES), jnp.float32),
        pltpu.VMEM((2, sources, LAGS, CH), jnp.float32),
        pltpu.VMEM((sources if clears else 1, LAGS, CH), jnp.float32),
        pltpu.SemaphoreType.DMA((2, -(-sources // PART))),
        pltpu.SemaphoreType.DMA((TILE_CAP,)),
    ]
    if first:
        out_shape.append(jax.ShapeDtypeStruct((CHUNKS, LAGS, LANES), jnp.bfloat16))
        out_specs = out_specs + [held]
    results = pl.pallas_call(
        functools.partial(tile_kernel, config),
        out_shape=out_shape,
        in_specs=specs,
        out_specs=out_specs,
        scratch_shapes=scratch_shapes,
        input_output_aliases={} if first else {len(operands) - 1: 0},
        compiler_params=pltpu.CompilerParams(vmem_limit_bytes=VMEM_BYTES),
        cost_estimate=pl.CostEstimate(
            flops=COSTS[phase - 1] * sources * CH * LAGS * 2 * FREQS,
            bytes_accessed=1024 * 1024,
            transcendentals=0,
        ),
        name="tiles{}".format(phase),
    )(*operands)
    return results if first else results[0]


def after_kernel(count, *refs):
    for i in range(count):
        refs[count + 2 + i][...] = refs[1 + i][...]


def after(out, *blocks):
    held = pl.BlockSpec(memory_space=pltpu.VMEM)
    anywhere = pl.BlockSpec(memory_space=pl.ANY)
    arrays = (out, *blocks)
    return pl.pallas_call(
        functools.partial(after_kernel, len(blocks)),
        out_shape=[jax.ShapeDtypeStruct(a.shape, a.dtype) for a in arrays],
        in_specs=[anywhere] + [held] * len(blocks),
        out_specs=[anywhere] + [held] * len(blocks),
        input_output_aliases={0: 0},
        compiler_params=pltpu.CompilerParams(vmem_limit_bytes=VMEM_BYTES),
        name="after",
    )(*arrays)


def paired_kernel(mine, other, out):
    out[0], out[1] = mine[...], other[...]


def paired(mine, other):
    return pl.pallas_call(
        paired_kernel,
        out_shape=jax.ShapeDtypeStruct((2, *mine.shape), mine.dtype),
        in_specs=[pl.BlockSpec(memory_space=pltpu.VMEM)] * 2,
        out_specs=pl.BlockSpec(memory_space=pltpu.VMEM),
        compiler_params=pltpu.CompilerParams(vmem_limit_bytes=VMEM_BYTES),
        name="paired",
    )(mine, other)


def per_device(samples, pair_tiles):
    devices = lax.axis_size("chan")
    members = lax.axis_size("win")
    windows = samples.shape[0] * members
    sources = VIRTUAL_SOURCES // members
    scale = 1.0 / math.sqrt(FREQS * windows)

    def arriving(block, *routes):
        pairs = []
        for i in range(devices):
            for w in range(members):
                j = i + routes[w % len(routes)][i % 4]
                if 0 <= j < devices:
                    pairs.append((j * members + w, i * members + w))
        return lax.ppermute(block, ("chan", "win"), pairs)

    def swapped(block):
        return lax.ppermute(block, "win", [(0, 1), (1, 0)])

    def gathered(block):
        return lax.all_gather(block, "win", axis=0)

    flip_x, flip_y = (1, -1, 1, -1), (2, 2, -2, -2)
    to_third, to_fourth = (-2, 2, -2, 2), (-4, -4, 4, 4)

    pairs = pair_tiles.T
    own = whiten(samples)
    call = functools.partial(tile_call, sources=sources, windows=windows, scale=scale)
    if members == 2:
        blocks = [own, swapped(own)]
        near = arriving(paired(*blocks), flip_x, flip_y)
        layout = ((0, "own", 2),)
        out, inverse = call(1, [pairs], layout, blocks, out=None)
        known = [pairs, inverse]
        out, near = after(out, near)
        far = arriving(near, to_third, to_fourth)
        blocks = blocks + [near, swapped(near)]
        layout = layout + ((1, "two", 2),)
        out = call(2, known, layout, blocks, out=out, clears=True)
        out, far = after(out, far)
        far = [far, swapped(far)]
        out = call(3, known, layout + ((FAR, "two", 1),), blocks + far[:1], out=out)
        return call(4, known, layout + ((FAR, "two", 2),), blocks + far, out=out)
    layout = tuple((place, "all", 1) for place in range(NEARBY))
    near = [arriving(own, flip_x), arriving(own, flip_y)]
    blocks = [gathered(own)]
    out, inverse = call(1, [pairs], layout[:1], blocks, out=None)
    known = [pairs, inverse]
    far = [arriving(near[0], to_third), arriving(near[1], to_fourth)]
    blocks = blocks + [gathered(block) for block in near]
    out = call(2, known, layout[:FAR], blocks, out=out, clears=True)
    blocks = blocks + [gathered(block) for block in far]
    return call(3, known, layout, blocks, out=out)


def solution(mesh):
    placed = (P("win", "chan", None), P())
    return jax.shard_map(
        per_device,
        mesh=mesh,
        in_specs=placed,
        out_specs=P("chan", "win", None, None),
        check_vma=False,
    )
```

profile of v0, /device:TPU:18, one launch (start us, length us, event | category | flops | bytes accessed | tf_op | source)
XLA Modules:
  0.0 38.4 jit_solution(7407812703884021205)
XLA Ops:
  0.0 0.6 %forward_table.1.table = bf16[4,256,256]{2,1,0:T(8,128)(2,1)S(1)} custom-call(), custom_call_target="tpu_custom_call" | custom-call | tf_op jit(solution)/shard_map/forward_table/pallas_call | solution.py:57
  0.6 0.0 copy-start
  0.6 0.9 %copy-done = bf16[1,128,1024]{2,1,0:T(8,128)(2,1)S(1)} copy-done((bf16[1,128,1024]{2,1,0:T(8,128)(2,1)S(1)}, bf16[1,128,1024]{2,1,0:T(8,128)(2,1)}, u32[]{:S(2)}) %copy-start) | copy-done | bytes 262168
  1.5 0.6 %whiten.1.refs_0_.mine.refs_1_ = bf16[8,128,128]{2,1,0:T(8,128)(2,1)S(1)} custom-call(bf16[1,128,1024]{2,1,0:T(8,128)(2,1)S(1)} %copy-done, bf16[4,256,256]{2,1,0:T(8,128)(2,1)S(1)} %forward_table.1.table), custom_call_target="tpu_custom_call" | custom-call | tf_op jit(solution)/shard_map/whiten/pallas_call | solution.py:128
  2.1 0.1 collective-permute-start
  2.2 1.5 %collective-permute-done.refs_1_.other.refs_2_ = bf16[8,128,128]{2,1,0:T(8,128)(2,1)S(1)} collective-permute-done((bf16[8,128,128]{2,1,0:T(8,128)(2,1)S(1)}, bf16[8,128,128]{2,1,0:T(8,128)(2,1)S(1)}, u32[]{:S(2)}, u32[]{:S(2)}) %collective-permute-start) | collective-permute-done | bytes 262176 | tf_op jit(solution)/shard_map/ppermute | solution.py:363
  3.7 0.6 %collective-permute-start.1 = (bf16[2,8,128,128]{3,2,1,0:T(8,128)(2,1)S(1)}, bf16[2,8,128,128]{3,2,1,0:T(8,128)(2,1)S(1)}, u32[]{:S(2)}, u32[]{:S(2)}) collective-permute-start(bf16[2,8,128,128]{3,2,1,0:T(8,128)(2,1)S(1)} %paired.1), channel_id=1, source_target_pairs={{2,0},{5,1},{0,2},{7,3},{6,4},{1,5},{4,6},{3,7},{10,8},{13,9},{8,1... | collective-permute-start | bytes 1572872 | tf_op jit(solution)/shard_map/ppermute | solution.py:360
  4.3 0.0 copy-start.1
  4.3 0.7 %copy-done.1 = s32[128,3]{0,1:T(4,128)S(1)} copy-done((s32[128,3]{0,1:T(4,128)S(1)}, s32[128,3]{0,1:T(4,128)}, u32[]{:S(2)}) %copy-start.1) | copy-done | bytes 1560
  5.0 3.8 %tiles1.1 = (f32[8,32,128,128]{3,2,1,0:T(8,128)}, bf16[8,128,128]{2,1,0:T(8,128)(2,1)S(1)}) custom-call(s32[3,128]{1,0:T(4,128)S(1)} %bitcast.1, bf16[8,128,128]{2,1,0:T(8,128)(2,1)S(1)} %whiten.1.refs_0_.mine.refs_1_, bf16[8,128,128]{2,1,0:T(8,128)(2,1)S(1)} %collective-permute-done.refs_1_.other.refs_2_), custom_call_target="tpu_custom_call" | custom-call | flops 536870912 | bytes 1048576 | tf_op jit(solution)/shard_map/tiles1/pallas_call | solution.py:293
  8.8 4.2 %collective-permute-done.1.refs_1_ = bf16[2,8,128,128]{3,2,1,0:T(8,128)(2,1)S(1)} collective-permute-done((bf16[2,8,128,128]{3,2,1,0:T(8,128)(2,1)S(1)}, bf16[2,8,128,128]{3,2,1,0:T(8,128)(2,1)S(1)}, u32[]{:S(2)}, u32[]{:S(2)}) %collective-permute-start.1) | collective-permute-done | bytes 524320 | tf_op jit(solution)/shard_map/ppermute | solution.py:360
  13.0 0.1 collective-permute-start.2
  13.1 3.5 %collective-permute-start.3 = (bf16[2,8,128,128]{3,2,1,0:T(8,128)(2,1)S(1)}, bf16[2,8,128,128]{3,2,1,0:T(8,128)(2,1)S(1)}, u32[]{:S(2)}, u32[]{:S(2)}) collective-permute-start(bf16[2,8,128,128]{3,2,1,0:T(8,128)(2,1)S(1)} %get-tuple-element.13.refs_3_), channel_id=1, source_target_pairs={{6,2},{0,4},{13,5},{10,6},{15,7},{4,8},{1,9},{14,10},{3,11},{8,12}... | collective-permute-start | bytes 1572872 | tf_op jit(solution)/shard_map/ppermute | solution.py:360
  16.6 0.0 collective-permute-done.2.refs_4_
  16.6 8.8 %tiles2.1.refs_0_ = f32[8,32,128,128]{3,2,1,0:T(8,128)} custom-call(s32[3,128]{1,0:T(4,128)S(1)} %bitcast.2, bf16[8,128,128]{2,1,0:T(8,128)(2,1)S(1)} %get-tuple-element.11.refs_0_, bf16[8,128,128]{2,1,0:T(8,128)(2,1)S(1)} %whiten.1.refs_0_.mine.refs_1_, ...), custom_call_target="tpu_custom_call", output_to_operand_aliasing={{}: (6, {})} | custom-call | flops 8589934592 | bytes 1048576 | tf_op jit(solution)/shard_map/tiles2/pallas_call | solution.py:293
  25.4 0.0 collective-permute-done.3.refs_1_
  25.5 0.4 %collective-permute-start.4 = (bf16[2,8,128,128]{3,2,1,0:T(8,128)(2,1)S(1)}, bf16[2,8,128,128]{3,2,1,0:T(8,128)(2,1)S(1)}, u32[]{:S(2)}, u32[]{:S(2)}) collective-permute-start(bf16[2,8,128,128]{3,2,1,0:T(8,128)(2,1)S(1)} %get-tuple-element.15.refs_5_), channel_id=1, source_target_pairs={{0,1},{1,0},{2,3},{3,2},{4,5},{5,4},{6,7},{7,6},{8,9},{9,8},{10,11... | collective-permute-start | bytes 1572872 | tf_op jit(solution)/shard_map/ppermute | solution.py:363
  25.9 6.2 %tiles3.1.refs_7_ = f32[8,32,128,128]{3,2,1,0:T(8,128)} custom-call(s32[3,128]{1,0:T(4,128)S(1)} %bitcast.3, bf16[8,128,128]{2,1,0:T(8,128)(2,1)S(1)} %get-tuple-element.11.refs_0_, bf16[8,128,128]{2,1,0:T(8,128)(2,1)S(1)} %whiten.1.refs_0_.mine.refs_1_, ...), custom_call_target="tpu_custom_call", output_to_operand_aliasing={{}: (7, {})} | custom-call | flops 8589934592 | bytes 1048576 | tf_op jit(solution)/shard_map/tiles3/pallas_call | solution.py:293
  32.1 0.0 collective-permute-done.4.refs_6_
  32.1 6.2 %tiles4.1 = f32[8,32,128,128]{3,2,1,0:T(8,128)} custom-call(s32[3,128]{1,0:T(4,128)S(1)} %bitcast.4, bf16[8,128,128]{2,1,0:T(8,128)(2,1)S(1)} %get-tuple-element.11.refs_0_, bf16[8,128,128]{2,1,0:T(8,128)(2,1)S(1)} %whiten.1.refs_0_.mine.refs_1_, bf16[8,128,128]{2,1,0:T(8,128)(2,1)S(1)} %collective-permute-done.refs_1_.other.refs_2_, ...), custom_call_target="tpu_custom_call", output_to_operand_aliasing={{}: (8, {})} | custom-call | flops 8589934592 | bytes 1048576 | tf_op jit(solution)/shard_map/tiles4/pallas_call | solution.py:293
  (3 shorter events, 0.1 us)
Async XLA Ops:
  0.6 1.0 %copy-start = (bf16[1,128,1024]{2,1,0:T(8,128)(2,1)S(1)}, bf16[1,128,1024]{2,1,0:T(8,128)(2,1)}, u32[]{:S(2)}) copy-start(bf16[1,128,1024]{2,1,0:T(8,128)(2,1)} %samples.1) | copy-start | bytes 786436
  2.1 1.6 %collective-permute-start = (bf16[8,128,128]{2,1,0:T(8,128)(2,1)S(1)}, bf16[8,128,128]{2,1,0:T(8,128)(2,1)S(1)}, u32[]{:S(2)}, u32[]{:S(2)}) collective-permute-start(bf16[8,128,128]{2,1,0:T(8,128)(2,1)S(1)} %whiten.1.refs_0_.mine.refs_1_), channel_id=1, source_target_pairs={{0,1},{1,0},{2,3},{3,2},{4,5},{5,4},{6,7},{7,6},{8,9},{9,8},{10,11... | collective-permute-start | bytes 786440 | tf_op jit(solution)/shard_map/ppermute | solution.py:363
  3.7 9.2 %collective-permute-start.1 = (bf16[2,8,128,128]{3,2,1,0:T(8,128)(2,1)S(1)}, bf16[2,8,128,128]{3,2,1,0:T(8,128)(2,1)S(1)}, u32[]{:S(2)}, u32[]{:S(2)}) collective-permute-start(bf16[2,8,128,128]{3,2,1,0:T(8,128)(2,1)S(1)} %paired.1), channel_id=1, source_target_pairs={{2,0},{5,1},{0,2},{7,3},{6,4},{1,5},{4,6},{3,7},{10,8},{13,9},{8,1... | collective-permute-start | bytes 1572872 | tf_op jit(solution)/shard_map/ppermute | solution.py:360
  4.3 0.7 %copy-start.1 = (s32[128,3]{0,1:T(4,128)S(1)}, s32[128,3]{0,1:T(4,128)}, u32[]{:S(2)}) copy-start(s32[128,3]{0,1:T(4,128)} %param.3) | copy-start | bytes 4612
  13.0 3.6 %collective-permute-start.2 = (bf16[2,8,128,128]{3,2,1,0:T(8,128)(2,1)S(1)}, bf16[2,8,128,128]{3,2,1,0:T(8,128)(2,1)S(1)}, u32[]{:S(2)}, u32[]{:S(2)}) collective-permute-start(bf16[2,8,128,128]{3,2,1,0:T(8,128)(2,1)S(1)} %get-tuple-element.13.refs_3_), channel_id=1, source_target_pairs={{0,1},{1,0},{2,3},{3,2},{4,5},{5,4},{6,7},{7,6},{8,9},{9,8},{10,11... | collective-permute-start | bytes 1572872 | tf_op jit(solution)/shard_map/ppermute | solution.py:363
  13.1 12.3 %collective-permute-start.3 = (bf16[2,8,128,128]{3,2,1,0:T(8,128)(2,1)S(1)}, bf16[2,8,128,128]{3,2,1,0:T(8,128)(2,1)S(1)}, u32[]{:S(2)}, u32[]{:S(2)}) collective-permute-start(bf16[2,8,128,128]{3,2,1,0:T(8,128)(2,1)S(1)} %get-tuple-element.13.refs_3_), channel_id=1, source_target_pairs={{6,2},{0,4},{13,5},{10,6},{15,7},{4,8},{1,9},{14,10},{3,11},{8,12}... | collective-permute-start | bytes 1572872 | tf_op jit(solution)/shard_map/ppermute | solution.py:360
  25.5 6.6 %collective-permute-start.4 = (bf16[2,8,128,128]{3,2,1,0:T(8,128)(2,1)S(1)}, bf16[2,8,128,128]{3,2,1,0:T(8,128)(2,1)S(1)}, u32[]{:S(2)}, u32[]{:S(2)}) collective-permute-start(bf16[2,8,128,128]{3,2,1,0:T(8,128)(2,1)S(1)} %get-tuple-element.15.refs_5_), channel_id=1, source_target_pairs={{0,1},{1,0},{2,3},{3,2},{4,5},{5,4},{6,7},{7,6},{8,9},{9,8},{10,11... | collective-permute-start | bytes 1572872 | tf_op jit(solution)/shard_map/ppermute | solution.py:363
where the time goes:
time: 39 us; the launch traced here: 38.4 us
  Pallas kernels  26.2 us (67%)
  waiting for transfers between devices  5.68 us (15%)
  starting transfers between devices  4.67 us (12%)
  local copies, waits for them, and re-layouts  1.63 us (4%)
    pallas_call x4, Pallas kernels, tile_call(): pl.pallas_call(functools.partial(tile_kernel, config), out_shape=out_shap...  24.9 us
    ppermute x2, waiting for transfers between devices, arriving(): return lax.ppermute(block, ('chan', 'win'), pairs)  4.15 us
    ppermute x2, starting transfers between devices, arriving(): return lax.ppermute(block, ('chan', 'win'), pairs)  4.09 us
    unnamed x4, local copies, waits for them, and re-layouts  1.63 us
    ppermute x3, waiting for transfers between devices, swapped(): return lax.ppermute(block, 'win', [(0, 1), (1, 0)])  1.53 us
  transfers between devices with their start and end apart: 5, of which 2 were waited for; matrix products, arithmetic and copies ran while one was open for 0% of the time, Pallas kernels for 49%

commit v1 on v0

--- a/solution.py
+++ b/solution.py
@@ -172,14 +172,20 @@
         return pltpu.make_async_copy(zeros, out.at[j], zero_sems.at[j])
 
     def each_empty(act):
-        @pl.loop(0, TILE_CAP)
-        def _(j):
-            @pl.when(code_of(j) == 0)
-            def _():
-                act(j)
+        @pl.when(code_of(TILE_CAP - 1) == 0)
+        def _():
+            @pl.loop(0, TILE_CAP)
+            def _(j):
+                @pl.when(code_of(j) == 0)
+                def _():
+                    act(j)
 
     if clears:
-        zeros[...] = jnp.zeros_like(zeros)
+
+        @pl.when(code_of(TILE_CAP - 1) == 0)
+        def _():
+            zeros[...] = jnp.zeros_like(zeros)
+
         each_empty(lambda j: clear(j).start())
 
     def each_window(place, act):

time: 39 us -> 40 us (1.026)
  the two profiles are of different devices: /device:TPU:18 before, /device:TPU:22 now
where the time goes in v1:
time: 40 us; the launch traced here: 40.3 us
  Pallas kernels  26.1 us (65%)
  waiting for transfers between devices  9.09 us (23%)
  starting transfers between devices  3.23 us (8%)
  local copies, waits for them, and re-layouts  1.63 us (4%)
    pallas_call x4, Pallas kernels, tile_call(): pl.pallas_call(functools.partial(tile_kernel, config), out_shape=out_shap...  24.9 us
    ppermute x2, waiting for transfers between devices, arriving(): return lax.ppermute(block, ('chan', 'win'), pairs)  7.56 us
    ppermute x2, starting transfers between devices, arriving(): return lax.ppermute(block, ('chan', 'win'), pairs)  3.02 us
    unnamed x4, local copies, waits for them, and re-layouts  1.63 us
    ppermute x3, waiting for transfers between devices, swapped(): return lax.ppermute(block, 'win', [(0, 1), (1, 0)])  1.53 us
  transfers between devices with their start and end apart: 5, of which 3 were waited for; matrix products, arithmetic and copies ran while one was open for 0% of the time, Pallas kernels for 46%

profile of v1, /device:TPU:22, one launch (start us, length us, event | category | flops | bytes accessed | tf_op | source)
XLA Modules:
  0.0 40.3 jit_solution(16323937319269944822)
XLA Ops:
  0.0 0.6 %forward_table.1.table = bf16[4,256,256]{2,1,0:T(8,128)(2,1)S(1)} custom-call(), custom_call_target="tpu_custom_call" | custom-call | tf_op jit(solution)/shard_map/forward_table/pallas_call | solution.py:57
  0.6 0.0 copy-start
  0.6 0.9 %copy-done = bf16[1,128,1024]{2,1,0:T(8,128)(2,1)S(1)} copy-done((bf16[1,128,1024]{2,1,0:T(8,128)(2,1)S(1)}, bf16[1,128,1024]{2,1,0:T(8,128)(2,1)}, u32[]{:S(2)}) %copy-start) | copy-done | bytes 262168
  1.5 0.6 %whiten.1.refs_0_.mine.refs_1_ = bf16[8,128,128]{2,1,0:T(8,128)(2,1)S(1)} custom-call(bf16[1,128,1024]{2,1,0:T(8,128)(2,1)S(1)} %copy-done, bf16[4,256,256]{2,1,0:T(8,128)(2,1)S(1)} %forward_table.1.table), custom_call_target="tpu_custom_call" | custom-call | tf_op jit(solution)/shard_map/whiten/pallas_call | solution.py:128
  2.1 0.1 collective-permute-start
  2.2 1.5 %collective-permute-done.refs_1_.other.refs_2_ = bf16[8,128,128]{2,1,0:T(8,128)(2,1)S(1)} collective-permute-done((bf16[8,128,128]{2,1,0:T(8,128)(2,1)S(1)}, bf16[8,128,128]{2,1,0:T(8,128)(2,1)S(1)}, u32[]{:S(2)}, u32[]{:S(2)}) %collective-permute-start) | collective-permute-done | bytes 262176 | tf_op jit(solution)/shard_map/ppermute | solution.py:369
  3.7 0.6 %collective-permute-start.1 = (bf16[2,8,128,128]{3,2,1,0:T(8,128)(2,1)S(1)}, bf16[2,8,128,128]{3,2,1,0:T(8,128)(2,1)S(1)}, u32[]{:S(2)}, u32[]{:S(2)}) collective-permute-start(bf16[2,8,128,128]{3,2,1,0:T(8,128)(2,1)S(1)} %paired.1), channel_id=1, source_target_pairs={{2,0},{5,1},{0,2},{7,3},{6,4},{1,5},{4,6},{3,7},{10,8},{13,9},{8,1... | collective-permute-start | bytes 1572872 | tf_op jit(solution)/shard_map/ppermute | solution.py:366
  4.3 0.0 copy-start.1
  4.3 0.7 %copy-done.1 = s32[128,3]{0,1:T(4,128)S(1)} copy-done((s32[128,3]{0,1:T(4,128)S(1)}, s32[128,3]{0,1:T(4,128)}, u32[]{:S(2)}) %copy-start.1) | copy-done | bytes 1560
  5.0 3.8 %tiles1.1 = (f32[8,32,128,128]{3,2,1,0:T(8,128)}, bf16[8,128,128]{2,1,0:T(8,128)(2,1)S(1)}) custom-call(s32[3,128]{1,0:T(4,128)S(1)} %bitcast.1, bf16[8,128,128]{2,1,0:T(8,128)(2,1)S(1)} %whiten.1.refs_0_.mine.refs_1_, bf16[8,128,128]{2,1,0:T(8,128)(2,1)S(1)} %collective-permute-done.refs_1_.other.refs_2_), custom_call_target="tpu_custom_call" | custom-call | flops 536870912 | bytes 1048576 | tf_op jit(solution)/shard_map/tiles1/pallas_call | solution.py:299
  8.8 4.2 %collective-permute-done.1.refs_1_ = bf16[2,8,128,128]{3,2,1,0:T(8,128)(2,1)S(1)} collective-permute-done((bf16[2,8,128,128]{3,2,1,0:T(8,128)(2,1)S(1)}, bf16[2,8,128,128]{3,2,1,0:T(8,128)(2,1)S(1)}, u32[]{:S(2)}, u32[]{:S(2)}) %collective-permute-start.1) | collective-permute-done | bytes 524320 | tf_op jit(solution)/shard_map/ppermute | solution.py:366
  13.0 0.1 collective-permute-start.2
  13.1 2.4 %collective-permute-start.3 = (bf16[2,8,128,128]{3,2,1,0:T(8,128)(2,1)S(1)}, bf16[2,8,128,128]{3,2,1,0:T(8,128)(2,1)S(1)}, u32[]{:S(2)}, u32[]{:S(2)}) collective-permute-start(bf16[2,8,128,128]{3,2,1,0:T(8,128)(2,1)S(1)} %get-tuple-element.13.refs_3_), channel_id=1, source_target_pairs={{6,2},{0,4},{13,5},{10,6},{15,7},{4,8},{1,9},{14,10},{3,11},{8,12}... | collective-permute-start | bytes 1572872 | tf_op jit(solution)/shard_map/ppermute | solution.py:366
  15.5 0.0 collective-permute-done.2.refs_4_
  15.5 6.1 %tiles2.1.refs_0_ = f32[8,32,128,128]{3,2,1,0:T(8,128)} custom-call(s32[3,128]{1,0:T(4,128)S(1)} %bitcast.2, bf16[8,128,128]{2,1,0:T(8,128)(2,1)S(1)} %get-tuple-element.11.refs_0_, bf16[8,128,128]{2,1,0:T(8,128)(2,1)S(1)} %whiten.1.refs_0_.mine.refs_1_, ...), custom_call_target="tpu_custom_call", output_to_operand_aliasing={{}: (6, {})} | custom-call | flops 8589934592 | bytes 1048576 | tf_op jit(solution)/shard_map/tiles2/pallas_call | solution.py:299
  21.7 3.4 %collective-permute-done.3.refs_1_ = bf16[2,8,128,128]{3,2,1,0:T(8,128)(2,1)S(1)} collective-permute-done((bf16[2,8,128,128]{3,2,1,0:T(8,128)(2,1)S(1)}, bf16[2,8,128,128]{3,2,1,0:T(8,128)(2,1)S(1)}, u32[]{:S(2)}, u32[]{:S(2)}) %collective-permute-start.3) | collective-permute-done | bytes 524320 | tf_op jit(solution)/shard_map/ppermute | solution.py:366
  25.1 0.1 collective-permute-start.4
  25.2 8.7 %tiles3.1.refs_7_ = f32[8,32,128,128]{3,2,1,0:T(8,128)} custom-call(s32[3,128]{1,0:T(4,128)S(1)} %bitcast.3, bf16[8,128,128]{2,1,0:T(8,128)(2,1)S(1)} %get-tuple-element.11.refs_0_, bf16[8,128,128]{2,1,0:T(8,128)(2,1)S(1)} %whiten.1.refs_0_.mine.refs_1_, ...), custom_call_target="tpu_custom_call", output_to_operand_aliasing={{}: (7, {})} | custom-call | flops 8589934592 | bytes 1048576 | tf_op jit(solution)/shard_map/tiles3/pallas_call | solution.py:299
  33.9 0.0 collective-permute-done.4.refs_6_
  33.9 6.2 %tiles4.1 = f32[8,32,128,128]{3,2,1,0:T(8,128)} custom-call(s32[3,128]{1,0:T(4,128)S(1)} %bitcast.4, bf16[8,128,128]{2,1,0:T(8,128)(2,1)S(1)} %get-tuple-element.11.refs_0_, bf16[8,128,128]{2,1,0:T(8,128)(2,1)S(1)} %whiten.1.refs_0_.mine.refs_1_, bf16[8,128,128]{2,1,0:T(8,128)(2,1)S(1)} %collective-permute-done.refs_1_.other.refs_2_, ...), custom_call_target="tpu_custom_call", output_to_operand_aliasing={{}: (8, {})} | custom-call | flops 8589934592 | bytes 1048576 | tf_op jit(solution)/shard_map/tiles4/pallas_call | solution.py:299
  (3 shorter events, 0.1 us)
Async XLA Ops:
  0.6 1.0 %copy-start = (bf16[1,128,1024]{2,1,0:T(8,128)(2,1)S(1)}, bf16[1,128,1024]{2,1,0:T(8,128)(2,1)}, u32[]{:S(2)}) copy-start(bf16[1,128,1024]{2,1,0:T(8,128)(2,1)} %samples.1) | copy-start | bytes 786436
  2.1 1.6 %collective-permute-start = (bf16[8,128,128]{2,1,0:T(8,128)(2,1)S(1)}, bf16[8,128,128]{2,1,0:T(8,128)(2,1)S(1)}, u32[]{:S(2)}, u32[]{:S(2)}) collective-permute-start(bf16[8,128,128]{2,1,0:T(8,128)(2,1)S(1)} %whiten.1.refs_0_.mine.refs_1_), channel_id=1, source_target_pairs={{0,1},{1,0},{2,3},{3,2},{4,5},{5,4},{6,7},{7,6},{8,9},{9,8},{10,11... | collective-permute-start | bytes 786440 | tf_op jit(solution)/shard_map/ppermute | solution.py:369
  3.7 9.2 %collective-permute-start.1 = (bf16[2,8,128,128]{3,2,1,0:T(8,128)(2,1)S(1)}, bf16[2,8,128,128]{3,2,1,0:T(8,128)(2,1)S(1)}, u32[]{:S(2)}, u32[]{:S(2)}) collective-permute-start(bf16[2,8,128,128]{3,2,1,0:T(8,128)(2,1)S(1)} %paired.1), channel_id=1, source_target_pairs={{2,0},{5,1},{0,2},{7,3},{6,4},{1,5},{4,6},{3,7},{10,8},{13,9},{8,1... | collective-permute-start | bytes 1572872 | tf_op jit(solution)/shard_map/ppermute | solution.py:366
  4.3 0.7 %copy-start.1 = (s32[128,3]{0,1:T(4,128)S(1)}, s32[128,3]{0,1:T(4,128)}, u32[]{:S(2)}) copy-start(s32[128,3]{0,1:T(4,128)} %param.3) | copy-start | bytes 4612
  13.0 2.5 %collective-permute-start.2 = (bf16[2,8,128,128]{3,2,1,0:T(8,128)(2,1)S(1)}, bf16[2,8,128,128]{3,2,1,0:T(8,128)(2,1)S(1)}, u32[]{:S(2)}, u32[]{:S(2)}) collective-permute-start(bf16[2,8,128,128]{3,2,1,0:T(8,128)(2,1)S(1)} %get-tuple-element.13.refs_3_), channel_id=1, source_target_pairs={{0,1},{1,0},{2,3},{3,2},{4,5},{5,4},{6,7},{7,6},{8,9},{9,8},{10,11... | collective-permute-start | bytes 1572872 | tf_op jit(solution)/shard_map/ppermute | solution.py:369
  13.1 12.0 %collective-permute-start.3 = (bf16[2,8,128,128]{3,2,1,0:T(8,128)(2,1)S(1)}, bf16[2,8,128,128]{3,2,1,0:T(8,128)(2,1)S(1)}, u32[]{:S(2)}, u32[]{:S(2)}) collective-permute-start(bf16[2,8,128,128]{3,2,1,0:T(8,128)(2,1)S(1)} %get-tuple-element.13.refs_3_), channel_id=1, source_target_pairs={{6,2},{0,4},{13,5},{10,6},{15,7},{4,8},{1,9},{14,10},{3,11},{8,12}... | collective-permute-start | bytes 1572872 | tf_op jit(solution)/shard_map/ppermute | solution.py:366
  25.1 8.8 %collective-permute-start.4 = (bf16[2,8,128,128]{3,2,1,0:T(8,128)(2,1)S(1)}, bf16[2,8,128,128]{3,2,1,0:T(8,128)(2,1)S(1)}, u32[]{:S(2)}, u32[]{:S(2)}) collective-permute-start(bf16[2,8,128,128]{3,2,1,0:T(8,128)(2,1)S(1)} %get-tuple-element.15.refs_5_), channel_id=1, source_target_pairs={{0,1},{1,0},{2,3},{3,2},{4,5},{5,4},{6,7},{7,6},{8,9},{9,8},{10,11... | collective-permute-start | bytes 1572872 | tf_op jit(solution)/shard_map/ppermute | solution.py:369
